TPU v7x, 256 devices: a whole 4x4x8 slice. The times are simulated.
256 devices in a mesh: grp: 16 (over z, core), seq: 16 (over x, y).
Axes of the slice: x: 4, y: 4, z: 8, core: 2. Of those that a mesh axis runs over, the one named last changes fastest.
Arguments:
- inputs: bfloat16 [16, 2048, 5120], P('grp', 'seq'), may hold values from -6 to 6
- queries: bfloat16 [16, 2048, 4096], P('grp', 'seq'), may hold values from -600 to 600, as said below
- keys: bfloat16 [16, 2048, 512], P('grp', 'seq'), may hold values from -6 to 6, as said below
- values: bfloat16 [16, 2048, 512], P('grp', 'seq'), may hold values from -6 to 6
- outputs: bfloat16 [16, 2048, 4096], P('grp', 'seq'), may hold values from -6 to 6
- upstream: bfloat16 [16, 2048, 4096], P('grp', 'seq'), may hold values from -6 to 6
- lengths: int32 [16, 8], P('grp'), may hold values from 1 to 1024, 2048 in all within a row
- tenants: int32 [16, 8], P('grp'), may hold values from 0 to 7
- adapter_down_maps: bfloat16 [5120, 128], replicated, may hold values from -0.078125 to 0.078125
- adapter_up_maps: bfloat16 [128, 512], replicated, may hold values from -1.5 to 1.5
Outputs:
- queries_gradient: bfloat16 [16, 2048, 4096], P('grp', 'seq')
- keys_gradient: bfloat16 [16, 2048, 512], P('grp', 'seq')
- values_gradient: bfloat16 [16, 2048, 512], P('grp', 'seq')
- down_map_gradient: float32 [5120, 128], replicated
- up_map_gradient: float32 [128, 512], replicated
Inputs may be any that keep to these rules, and one draw needn't show every extreme that they name: `keys`: keys of order one. `queries`: queries of order one or more.
All inputs are finite; a program needn't handle non-finite values.
Results may differ from a plain program's by a relative error of at most 0.015.
Values may be sent and summed in bfloat16 or wider, within the bound.
No kernel may reach another device: no remote copies, remote signals or barrier semaphores. Data moves between devices by JAX's collectives and lax.ppermute only.
A program may use at most 64 MiB of HBM per device.

v0:
```python
import jax
import jax.numpy as jnp
from jax import lax
from jax.sharding import PartitionSpec as P

HEAD_SIZE = 128
ADAPTER_RANK = 16


adapter_scale = 2.0


def segment_ids(lengths, positions):
    ends = jnp.cumsum(lengths)
    return jnp.sum((positions[:, None] >= ends[None, :]).astype(jnp.int32), axis=1)


def tenant_ids(segments, tenants):
    docs = jnp.arange(tenants.shape[0], dtype=jnp.int32)
    return jnp.sum(jnp.where(segments[:, None] == docs[None, :], tenants[None, :], 0), axis=1)


def per_device(
    inputs,
    queries,
    keys,
    values,
    outputs,
    upstream,
    lengths,
    tenants,
    adapter_down_maps,
    adapter_up_maps,
):
    scale = HEAD_SIZE ** (-0.5)
    tok = queries.shape[1]
    slots = lax.axis_size("seq")
    q_count = queries.shape[2] // HEAD_SIZE
    kv_count = keys.shape[2] // HEAD_SIZE
    per_tenant_slot = q_count // slots
    q_slots = queries[0].reshape(tok, slots, per_tenant_slot * HEAD_SIZE)
    u_slots = upstream[0].reshape(tok, slots, per_tenant_slot * HEAD_SIZE)
    k_slots = jnp.repeat(keys[0].reshape(tok, kv_count, HEAD_SIZE), slots // kv_count, axis=1)
    v_slots = jnp.repeat(values[0].reshape(tok, kv_count, HEAD_SIZE), slots // kv_count, axis=1)
    span = tok * slots
    o_slots = outputs[0].reshape(tok, slots, per_tenant_slot * HEAD_SIZE)
    q_here, o_here, u_here, k_here, v_here = (
        lax.all_to_all(q_slots, "seq", split_axis=1, concat_axis=0, tiled=True),
        lax.all_to_all(o_slots, "seq", split_axis=1, concat_axis=0, tiled=True),
        lax.all_to_all(u_slots, "seq", split_axis=1, concat_axis=0, tiled=True),
        lax.all_to_all(k_slots, "seq", split_axis=1, concat_axis=0, tiled=True),
        lax.all_to_all(v_slots, "seq", split_axis=1, concat_axis=0, tiled=True),
    )
    deltas = jnp.sum(
        u_here.reshape(span, per_tenant_slot, HEAD_SIZE).astype(jnp.float32)
        * o_here.reshape(span, per_tenant_slot, HEAD_SIZE).astype(jnp.float32),
        axis=2,
    )
    key_slot = k_here.reshape(span, HEAD_SIZE)
    value_slot = v_here.reshape(span, HEAD_SIZE)
    segments = segment_ids(lengths[0], jnp.arange(span, dtype=jnp.int32))
    block_rows = min(512, span)
    blocks = span // block_rows
    key_index = jnp.arange(span, dtype=jnp.int32)
    row_index = jnp.arange(block_rows, dtype=jnp.int32)
    block_items = (
        q_here.reshape(blocks, block_rows, per_tenant_slot, HEAD_SIZE),
        u_here.reshape(blocks, block_rows, per_tenant_slot, HEAD_SIZE),
        deltas.reshape(blocks, block_rows, per_tenant_slot),
        segments.reshape(blocks, block_rows),
        jnp.arange(blocks, dtype=jnp.int32) * block_rows,
    )

    def block_step(carry, items):
        key_acc, value_acc = carry
        q_block, u_block, d_block, s_block, first = items
        scores = (
            jnp.einsum("qhd,kd->hqk", q_block, key_slot, preferred_element_type=jnp.float32) * scale
        )
        allowed = (s_block[:, None] == segments[None, :]) & (
            key_index[None, :] <= (first + row_index)[:, None]
        )
        masked = jnp.where(allowed[None], scores, -jnp.inf)
        top = jnp.max(masked, axis=2, keepdims=True)
        weights = jnp.exp(masked - top)
        prob = weights / jnp.sum(weights, axis=2, keepdims=True)
        dprob = jnp.einsum("qhd,kd->hqk", u_block, value_slot, preferred_element_type=jnp.float32)
        dscore = (prob * (dprob - jnp.transpose(d_block)[:, :, None])).astype(jnp.bfloat16)
        dquery = (
            jnp.einsum("hqk,kd->qhd", dscore, key_slot, preferred_element_type=jnp.float32) * scale
        ).astype(jnp.bfloat16)
        key_acc = (
            key_acc
            + jnp.einsum("hqk,qhd->kd", dscore, q_block, preferred_element_type=jnp.float32) * scale
        )
        value_acc = value_acc + jnp.einsum(
            "hqk,qhd->kd", prob.astype(jnp.bfloat16), u_block, preferred_element_type=jnp.float32
        )
        return ((key_acc, value_acc), dquery)

    empty = jnp.zeros((span, HEAD_SIZE), jnp.float32)
    (key_part, value_part), dquery = lax.scan(block_step, (empty, empty), block_items)
    dquery = dquery.reshape(span, 1, per_tenant_slot * HEAD_SIZE)
    dquery = lax.all_to_all(dquery, "seq", split_axis=0, concat_axis=1, tiled=True)
    queries_gradient = dquery.reshape(1, tok, q_count * HEAD_SIZE)
    key_short = key_part.astype(jnp.bfloat16).reshape(span, 1, HEAD_SIZE)
    value_short = value_part.astype(jnp.bfloat16).reshape(span, 1, HEAD_SIZE)
    key_back, value_back = (
        lax.all_to_all(key_short, "seq", split_axis=0, concat_axis=1, tiled=True),
        lax.all_to_all(value_short, "seq", split_axis=0, concat_axis=1, tiled=True),
    )
    keys_gradient = jnp.sum(
        key_back.astype(jnp.float32).reshape(tok, kv_count, slots // kv_count, HEAD_SIZE), axis=2
    ).astype(jnp.bfloat16)
    values_gradient = jnp.sum(
        value_back.astype(jnp.float32).reshape(tok, kv_count, slots // kv_count, HEAD_SIZE), axis=2
    ).astype(jnp.bfloat16)
    keys_gradient = keys_gradient.reshape(1, tok, kv_count * HEAD_SIZE)
    flattened_values = values_gradient.reshape(tok, kv_count * HEAD_SIZE)
    values_gradient = flattened_values.reshape(1, tok, kv_count * HEAD_SIZE)
    positions = lax.axis_index("seq") * tok + jnp.arange(tok, dtype=jnp.int32)
    owners = tenant_ids(segment_ids(lengths[0], positions), tenants[0])
    column_indices = jnp.arange(adapter_down_maps.shape[1], dtype=jnp.int32) // ADAPTER_RANK
    owned = column_indices[None, :] == owners[:, None]
    low_rank_state = jnp.dot(inputs[0], adapter_down_maps, preferred_element_type=jnp.float32)
    low_rank_state = jnp.where(owned, low_rank_state, 0.0).astype(jnp.bfloat16)
    backward_pass = (
        jnp.dot(flattened_values, adapter_up_maps.T, preferred_element_type=jnp.float32)
        * adapter_scale
    )
    backward_pass = jnp.where(owned, backward_pass, 0.0).astype(jnp.bfloat16)
    down_portion = jnp.dot(inputs[0].T, backward_pass, preferred_element_type=jnp.float32)
    up_portion = (
        jnp.dot(low_rank_state.T, flattened_values, preferred_element_type=jnp.float32)
        * adapter_scale
    )
    down_map_gradient, up_map_gradient = lax.psum((down_portion, up_portion), ("grp", "seq"))
    return (queries_gradient, keys_gradient, values_gradient, down_map_gradient, up_map_gradient)


def solution(mesh):
    in_specs = (
        P("grp", "seq", None),
        P("grp", "seq", None),
        P("grp", "seq", None),
        P("grp", "seq", None),
        P("grp", "seq", None),
        P("grp", "seq", None),
        P("grp", None),
        P("grp", None),
        P(),
        P(),
    )
    out_specs = (P("grp", "seq", None), P("grp", "seq", None), P("grp", "seq", None), P(), P())
    return jax.shard_map(
        per_device, mesh=mesh, in_specs=in_specs, out_specs=out_specs, check_vma=False
    )
```

profile of v0, /device:TPU:2, one launch (start us, length us, event | category | flops | bytes accessed | tf_op | source)
XLA Modules:
  0.0 518.1 jit_solution(14955212187547509413)
XLA Ops:
  9.2 7.5 %all-to-all-start.3 = ((bf16[128,16,128]{2,0,1:T(8,128)(2,1)}), bf16[128,16,128]{2,0,1:T(8,128)(2,1)S(1)}, u32[]{:S(2)}, u32[]{:S(2)}) async-start(bf16[128,16,128]{2,0,1:T(8,128)(2,1)} %bitcast.11), calls=%async_computation.3 | async-start | bytes 1048576 | tf_op jit(solution)/shard_map/all_to_all | solution.py:52
  16.7 2.3 copy.93
  18.9 7.1 %all-to-all-done.3 = bf16[128,16,128]{2,0,1:T(8,128)(2,1)S(1)} async-done(((bf16[128,16,128]{2,0,1:T(8,128)(2,1)}), bf16[128,16,128]{2,0,1:T(8,128)(2,1)S(1)}, u32[]{:S(2)}, u32[]{:S(2)}) %all-to-all-start.3) | async-done | bytes 524320 | tf_op jit(solution)/shard_map/all_to_all | solution.py:52
  26.8 5.7 %all-to-all-start.2 = ((bf16[128,16,256]{0,2,1:T(8,128)(2,1)}), bf16[128,16,256]{0,2,1:T(8,128)(2,1)S(1)}, u32[]{:S(2)}, u32[]{:S(2)}) async-start(bf16[128,16,256]{0,2,1:T(8,128)(2,1)} %bitcast.8), calls=%async_computation.2 | async-start | bytes 2097152 | tf_op jit(solution)/shard_map/all_to_all | solution.py:50
  33.9 12.6 %all-to-all-done.2 = bf16[128,16,256]{0,2,1:T(8,128)(2,1)S(1)} async-done(((bf16[128,16,256]{0,2,1:T(8,128)(2,1)}), bf16[128,16,256]{0,2,1:T(8,128)(2,1)S(1)}, u32[]{:S(2)}, u32[]{:S(2)}) %all-to-all-start.2) | async-done | bytes 1048608 | tf_op jit(solution)/shard_map/all_to_all | solution.py:50
  46.5 5.8 %all-to-all-start.4 = ((bf16[128,16,256]{0,2,1:T(8,128)(2,1)}), bf16[128,16,256]{0,2,1:T(8,128)(2,1)S(1)}, u32[]{:S(2)}, u32[]{:S(2)}) async-start(bf16[128,16,256]{0,2,1:T(8,128)(2,1)} %bitcast.16), calls=%async_computation.4 | async-start | bytes 2097152 | tf_op jit(solution)/shard_map/all_to_all | solution.py:49
  55.1 11.0 %all-to-all-done.4 = bf16[128,16,256]{0,2,1:T(8,128)(2,1)S(1)} async-done(((bf16[128,16,256]{0,2,1:T(8,128)(2,1)}), bf16[128,16,256]{0,2,1:T(8,128)(2,1)S(1)}, u32[]{:S(2)}, u32[]{:S(2)}) %all-to-all-start.4) | async-done | bytes 1048608 | tf_op jit(solution)/shard_map/all_to_all | solution.py:49
  67.1 5.5 %all-to-all-start = ((bf16[128,16,256]{2,0,1:T(8,128)(2,1)}), bf16[128,16,256]{2,0,1:T(8,128)(2,1)S(1)}, u32[]{:S(2)}, u32[]{:S(2)}) async-start(bf16[128,16,256]{2,0,1:T(8,128)(2,1)} %copy.91), calls=%async_computation | async-start | bytes 2097152 | tf_op jit(solution)/shard_map/all_to_all | solution.py:48
  74.4 12.1 %all-to-all-done = bf16[128,16,256]{2,0,1:T(8,128)(2,1)S(1)} async-done(((bf16[128,16,256]{2,0,1:T(8,128)(2,1)}), bf16[128,16,256]{2,0,1:T(8,128)(2,1)S(1)}, u32[]{:S(2)}, u32[]{:S(2)}) %all-to-all-start) | async-done | bytes 1048608 | tf_op jit(solution)/shard_map/all_to_all | solution.py:48
  87.5 6.0 %all-to-all-start.1 = ((bf16[128,16,128]{2,0,1:T(8,128)(2,1)}), bf16[128,16,128]{2,0,1:T(8,128)(2,1)}, u32[]{:S(2)}, u32[]{:S(2)}) async-start(bf16[128,16,128]{2,0,1:T(8,128)(2,1)} %bitcast.201), calls=%async_computation.1 | async-start | bytes 1048576 | tf_op jit(solution)/shard_map/all_to_all | solution.py:51
  95.1 2.5 copy.97
  97.7 2.7 mul.44
  101.7 2.2 reshape.212
  103.9 2.1 reshape.209
  107.8 100.2 %while.15 = (s32[]{:T(128)}, f32[2048,128]{1,0:T(8,128)S(1)}, f32[2048,128]{1,0:T(8,128)}, bf16[4,512,2,128]{3,2,1,0:T(2,128)(2,1)}, s32[4,512]{1,0:T(4,128)S(1)...) while((s32[]{:T(128)}, f32[2048,128]{1,0:T(8,128)S(1)}, ...), condition=%wide.region_6.7_spmd.clone, body=%wide.region_3.6_spmd.clone.sunk | while | flops 2710047232 | bytes 86289176 | solution.py:102
  110.4 2.2 constant_dynamic-slice_fusion.6
  112.6 7.4 %fusion.96 = (f32[2,512]{1,0:T(2,128)S(1)}, f32[2,512,2048]{2,1,0:T(8,128)}) fusion(pred[512,2048]{1,0:T(8,128)(4,1)S(1)} %fusion.95, bf16[2048,128]{1,0:T(8,128)(2,1)} %get-tuple-element.364, bf16[1,512,2,128]{3,2,1,0:T(2,128)(2,1)} %get-tuple-element.324), kind=kOutput, calls=%fused_computation.80.clone.1 | convolution fusion | flops 545261568 | bytes 10227712 | tf_op jit(solution)/shard_map/while/body/eval_jaxpr/sub | solution.py:85
  119.9 6.1 %fusion.99 = f32[2048,128]{1,0:T(8,128)} fusion(f32[2,512,2048]{2,1,0:T(8,128)} %get-tuple-element.325, f32[2,512]{1,0:T(2,128)S(1)} %get-tuple-element.326, f32[2048,128]{1,0:T(8,128)} %get-tuple-element.344, pred[]{:T(512)S(6)} %compare.7, bf16[1,512,2,128]{3,2,1,0:T(2,128)(2,1)} %get-tuple-element.327), kind=kOutput, calls=%fused_computation.23.clone.1 | convolution fusion | flops 541589504 | bytes 10752001 | tf_op jit(solution)/shard_map/while/body/eval_jaxpr/hqk,qhd->kd/dot_general | solution.py:96
  127.6 2.3 fusion.100
  130.9 1.8 fusion.98
  135.2 2.2 constant_dynamic-slice_fusion.6
  137.3 7.4 %fusion.96 = (f32[2,512]{1,0:T(2,128)S(1)}, f32[2,512,2048]{2,1,0:T(8,128)}) fusion(pred[512,2048]{1,0:T(8,128)(4,1)S(1)} %fusion.95, bf16[2048,128]{1,0:T(8,128)(2,1)} %get-tuple-element.364, bf16[1,512,2,128]{3,2,1,0:T(2,128)(2,1)} %get-tuple-element.324), kind=kOutput, calls=%fused_computation.80.clone.1 | convolution fusion | flops 545261568 | bytes 10227712 | tf_op jit(solution)/shard_map/while/body/eval_jaxpr/sub | solution.py:85
  144.7 6.4 %fusion.99 = f32[2048,128]{1,0:T(8,128)} fusion(f32[2,512,2048]{2,1,0:T(8,128)} %get-tuple-element.325, f32[2,512]{1,0:T(2,128)S(1)} %get-tuple-element.326, f32[2048,128]{1,0:T(8,128)} %get-tuple-element.344, pred[]{:T(512)S(6)} %compare.7, bf16[1,512,2,128]{3,2,1,0:T(2,128)(2,1)} %get-tuple-element.327), kind=kOutput, calls=%fused_computation.23.clone.1 | convolution fusion | flops 541589504 | bytes 10752001 | tf_op jit(solution)/shard_map/while/body/eval_jaxpr/hqk,qhd->kd/dot_general | solution.py:96
  152.7 2.3 fusion.100
  156.0 1.8 fusion.98
  160.3 2.2 constant_dynamic-slice_fusion.6
  162.4 7.4 %fusion.96 = (f32[2,512]{1,0:T(2,128)S(1)}, f32[2,512,2048]{2,1,0:T(8,128)}) fusion(pred[512,2048]{1,0:T(8,128)(4,1)S(1)} %fusion.95, bf16[2048,128]{1,0:T(8,128)(2,1)} %get-tuple-element.364, bf16[1,512,2,128]{3,2,1,0:T(2,128)(2,1)} %get-tuple-element.324), kind=kOutput, calls=%fused_computation.80.clone.1 | convolution fusion | flops 545261568 | bytes 10227712 | tf_op jit(solution)/shard_map/while/body/eval_jaxpr/sub | solution.py:85
  169.8 6.4 %fusion.99 = f32[2048,128]{1,0:T(8,128)} fusion(f32[2,512,2048]{2,1,0:T(8,128)} %get-tuple-element.325, f32[2,512]{1,0:T(2,128)S(1)} %get-tuple-element.326, f32[2048,128]{1,0:T(8,128)} %get-tuple-element.344, pred[]{:T(512)S(6)} %compare.7, bf16[1,512,2,128]{3,2,1,0:T(2,128)(2,1)} %get-tuple-element.327), kind=kOutput, calls=%fused_computation.23.clone.1 | convolution fusion | flops 541589504 | bytes 10752001 | tf_op jit(solution)/shard_map/while/body/eval_jaxpr/hqk,qhd->kd/dot_general | solution.py:96
  177.8 2.3 fusion.100
  181.1 1.8 fusion.98
  185.4 2.2 constant_dynamic-slice_fusion.6
  187.5 7.4 %fusion.96 = (f32[2,512]{1,0:T(2,128)S(1)}, f32[2,512,2048]{2,1,0:T(8,128)}) fusion(pred[512,2048]{1,0:T(8,128)(4,1)S(1)} %fusion.95, bf16[2048,128]{1,0:T(8,128)(2,1)} %get-tuple-element.364, bf16[1,512,2,128]{3,2,1,0:T(2,128)(2,1)} %get-tuple-element.324), kind=kOutput, calls=%fused_computation.80.clone.1 | convolution fusion | flops 545261568 | bytes 10227712 | tf_op jit(solution)/shard_map/while/body/eval_jaxpr/sub | solution.py:85
  194.9 6.4 %fusion.99 = f32[2048,128]{1,0:T(8,128)} fusion(f32[2,512,2048]{2,1,0:T(8,128)} %get-tuple-element.325, f32[2,512]{1,0:T(2,128)S(1)} %get-tuple-element.326, f32[2048,128]{1,0:T(8,128)} %get-tuple-element.344, pred[]{:T(512)S(6)} %compare.7, bf16[1,512,2,128]{3,2,1,0:T(2,128)(2,1)} %get-tuple-element.327), kind=kOutput, calls=%fused_computation.23.clone.1 | convolution fusion | flops 541589504 | bytes 10752001 | tf_op jit(solution)/shard_map/while/body/eval_jaxpr/hqk,qhd->kd/dot_general | solution.py:96
  202.9 2.3 fusion.100
  206.2 1.8 fusion.98
  211.8 7.3 %all-to-all-start.7 = ((bf16[16,2,8192]{2,1,0:T(2,128)(2,1)}), bf16[16,2,8192]{2,1,0:T(2,128)(2,1)S(1)}, u32[]{:S(2)}, u32[]{:S(2)}) async-start(bf16[16,2,8192]{2,1,0:T(2,128)(2,1)} %reshape.230), calls=%async_computation.7 | async-start | bytes 1048576 | tf_op jit(solution)/shard_map/all_to_all | solution.py:110
  221.3 5.7 %all-to-all-done.7 = bf16[16,2,8192]{2,1,0:T(2,128)(2,1)S(1)} async-done(((bf16[16,2,8192]{2,1,0:T(2,128)(2,1)}), bf16[16,2,8192]{2,1,0:T(2,128)(2,1)S(1)}, u32[]{:S(2)}, u32[]{:S(2)}) %all-to-all-start.7) | async-done | bytes 524320 | tf_op jit(solution)/shard_map/all_to_all | solution.py:110
  227.0 6.3 %all-to-all-start.6 = ((bf16[16,2,8192]{2,1,0:T(2,128)(2,1)}), bf16[16,2,8192]{2,1,0:T(2,128)(2,1)}, u32[]{:S(2)}, u32[]{:S(2)}) async-start(bf16[16,2,8192]{2,1,0:T(2,128)(2,1)} %reshape.228), calls=%async_computation.6 | async-start | bytes 1048576 | tf_op jit(solution)/shard_map/all_to_all | solution.py:109
  234.4 3.3 convolution_bitcast_fusion.1
  239.1 6.4 %reshape.225 = bf16[2048,1,256]{2,1,0:T(2,128)(2,1)S(1)} reshape(bf16[4,512,2,128]{3,2,1,0:T(2,128)(2,1)} %get-tuple-element.79) | data formatting | bytes 2097152 | tf_op jit(solution)/shard_map/reshape | solution.py:103
  245.5 11.6 %reduce.2 = bf16[2048,256]{1,0:T(8,128)(2,1)} reduce(bf16[2048,1,256]{2,1,0:T(2,128)(2,1)S(1)} %reshape.225, bf16[]{:T(256)} %broadcast.125), dimensions={1}, to_apply=%reshape.225.reduce_sub_computation | reduce | bytes 2097154 | tf_op jit(solution)/shard_map/reshape | solution.py:103
  257.1 2.2 reshape.226
  259.2 7.3 %all-to-all-start.5 = ((bf16[16,2,16384]{2,1,0:T(2,128)(2,1)}), bf16[16,2,16384]{2,1,0:T(2,128)(2,1)}, u32[]{:S(2)}, u32[]{:S(2)}) async-start(bf16[16,2,16384]{2,1,0:T(2,128)(2,1)} %reshape.226), calls=%async_computation.5 | async-start | bytes 2097152 | tf_op jit(solution)/shard_map/all_to_all | solution.py:104
  267.3 2.2 reshape.229
  270.6 8.2 %all-to-all-done.5 = bf16[16,2,16384]{2,1,0:T(2,128)(2,1)} async-done(((bf16[16,2,16384]{2,1,0:T(2,128)(2,1)}), bf16[16,2,16384]{2,1,0:T(2,128)(2,1)}, u32[]{:S(2)}, u32[]{:S(2)}) %all-to-all-start.5) | async-done | bytes 1048608 | tf_op jit(solution)/shard_map/all_to_all | solution.py:104
  278.8 4.3 reshape.227
  287.2 220.0 %all-reduce.3.cloned.1.call-done = (f32[5120,128]{0,1:T(8,128)}, f32[128,512]{1,0:T(8,128)}) async-done(((f32[5120,128]{0,1:T(8,128)}, f32[128,512]{1,0:T(8,128)}), (f32[5120,128]{0,1:T(8,128)}, f32[128,512]{1,0:T(8,128)})) %all-reduce.3.cloned.1.call-update) | async-done | bytes 2883600 | tf_op jit(solution)/shard_map/psum | solution.py:137
  507.3 3.3 copy.112
  (131 shorter events, 50.3 us)
Async XLA Ops:
  7.2 227.3 %copy-start = (bf16[1,128,5120]{2,1,0:T(8,128)(2,1)S(1)}, bf16[1,128,5120]{2,1,0:T(8,128)(2,1)}, u32[]{:S(2)}) copy-start(bf16[1,128,5120]{2,1,0:T(8,128)(2,1)} %param.12) | copy-start | bytes 3932164
  7.2 25.4 %copy-start.6 = (bf16[1,128,4096]{2,1,0:T(8,128)(2,1)S(1)}, bf16[1,128,4096]{2,1,0:T(8,128)(2,1)}, u32[]{:S(2)}) copy-start(bf16[1,128,4096]{2,1,0:T(8,128)(2,1)} %param.16) | copy-start | bytes 3145732
  9.2 16.8 %all-to-all-start.3 = ((bf16[128,16,128]{2,0,1:T(8,128)(2,1)}), bf16[128,16,128]{2,0,1:T(8,128)(2,1)S(1)}, u32[]{:S(2)}, u32[]{:S(2)}) async-start(bf16[128,16,128]{2,0,1:T(8,128)(2,1)} %bitcast.11), calls=%async_computation.3 | async-start | bytes 1048576 | tf_op jit(solution)/shard_map/all_to_all | solution.py:52
  26.0 0.8 copy-start.7
  26.8 19.7 %all-to-all-start.2 = ((bf16[128,16,256]{0,2,1:T(8,128)(2,1)}), bf16[128,16,256]{0,2,1:T(8,128)(2,1)S(1)}, u32[]{:S(2)}, u32[]{:S(2)}) async-start(bf16[128,16,256]{0,2,1:T(8,128)(2,1)} %bitcast.8), calls=%async_computation.2 | async-start | bytes 2097152 | tf_op jit(solution)/shard_map/all_to_all | solution.py:50
  46.5 26.0 %copy-start.10 = (bf16[1,128,512]{2,1,0:T(8,128)(2,1)S(1)}, bf16[1,128,512]{2,1,0:T(8,128)(2,1)}, u32[]{:S(2)}) copy-start(bf16[1,128,512]{2,1,0:T(8,128)(2,1)} %param.14) | copy-start | bytes 393220
  46.5 27.7 %copy-start.13 = (s32[1,8]{1,0:T(1,128)S(1)}, s32[1,8]{1,0:T(1,128)}, u32[]{:S(2)}) copy-start(s32[1,8]{1,0:T(1,128)} %param.18) | copy-start | bytes 100
  46.5 19.6 %all-to-all-start.4 = ((bf16[128,16,256]{0,2,1:T(8,128)(2,1)}), bf16[128,16,256]{0,2,1:T(8,128)(2,1)S(1)}, u32[]{:S(2)}, u32[]{:S(2)}) async-start(bf16[128,16,256]{0,2,1:T(8,128)(2,1)} %bitcast.16), calls=%async_computation.4 | async-start | bytes 2097152 | tf_op jit(solution)/shard_map/all_to_all | solution.py:49
  66.1 1.0 copy-start.4
  67.1 19.4 %all-to-all-start = ((bf16[128,16,256]{2,0,1:T(8,128)(2,1)}), bf16[128,16,256]{2,0,1:T(8,128)(2,1)S(1)}, u32[]{:S(2)}, u32[]{:S(2)}) async-start(bf16[128,16,256]{2,0,1:T(8,128)(2,1)} %copy.91), calls=%async_computation | async-start | bytes 2097152 | tf_op jit(solution)/shard_map/all_to_all | solution.py:48
  74.4 23.3 %copy-start.11 = (s32[8,1]{0,1:T(1,128)}, s32[8,1]{0,1:T(1,128)S(1)}, u32[]{:S(2)}) copy-start(s32[8,1]{0,1:T(1,128)S(1)} %reduce-window.8) | copy-start | bytes 100
  86.5 7.0 %copy-start.3 = (bf16[128,16,256]{2,0,1:T(8,128)(2,1)}, bf16[128,16,256]{2,0,1:T(8,128)(2,1)S(1)}, u32[]{:S(2)}) copy-start(bf16[128,16,256]{2,0,1:T(8,128)(2,1)S(1)} %all-to-all-done) | copy-start | bytes 3145732
  87.5 20.2 %all-to-all-start.1 = ((bf16[128,16,128]{2,0,1:T(8,128)(2,1)}), bf16[128,16,128]{2,0,1:T(8,128)(2,1)}, u32[]{:S(2)}, u32[]{:S(2)}) async-start(bf16[128,16,128]{2,0,1:T(8,128)(2,1)} %bitcast.201), calls=%async_computation.1 | async-start | bytes 1048576 | tf_op jit(solution)/shard_map/all_to_all | solution.py:51
  119.9 6.1 %copy-start.2 = (bf16[1,512,2,128]{3,2,1,0:T(2,128)(2,1)S(1)}, bf16[1,512,2,128]{3,2,1,0:T(2,128)(2,1)}, u32[]{:S(2)}) copy-start(bf16[1,512,2,128]{3,2,1,0:T(2,128)(2,1)} %get-tuple-element.327) | copy-start | bytes 786436 | tf_op jit(solution)/shard_map/while
  119.9 6.1 %copy-start.8 = (bf16[2048,128]{1,0:T(8,128)(2,1)S(1)}, bf16[2048,128]{1,0:T(8,128)(2,1)}, u32[]{:S(2)}) copy-start(bf16[2048,128]{1,0:T(8,128)(2,1)} %get-tuple-element.366) | copy-start | bytes 1572868 | tf_op jit(solution)/shard_map/while
  119.9 6.1 %copy-start.15 = (f32[2,512,2048]{2,1,0:T(8,128)S(1)}, f32[2,512,2048]{2,1,0:T(8,128)}, u32[]{:S(2)}) copy-start(f32[2,512,2048]{2,1,0:T(8,128)} %get-tuple-element.325) | copy-start | bytes 25165828 | tf_op jit(solution)/shard_map/while
  127.6 3.3 copy-start.1
  144.7 6.4 %copy-start.2 = (bf16[1,512,2,128]{3,2,1,0:T(2,128)(2,1)S(1)}, bf16[1,512,2,128]{3,2,1,0:T(2,128)(2,1)}, u32[]{:S(2)}) copy-start(bf16[1,512,2,128]{3,2,1,0:T(2,128)(2,1)} %get-tuple-element.327) | copy-start | bytes 786436 | tf_op jit(solution)/shard_map/while
  144.7 6.4 %copy-start.8 = (bf16[2048,128]{1,0:T(8,128)(2,1)S(1)}, bf16[2048,128]{1,0:T(8,128)(2,1)}, u32[]{:S(2)}) copy-start(bf16[2048,128]{1,0:T(8,128)(2,1)} %get-tuple-element.366) | copy-start | bytes 1572868 | tf_op jit(solution)/shard_map/while
  144.7 6.4 %copy-start.15 = (f32[2,512,2048]{2,1,0:T(8,128)S(1)}, f32[2,512,2048]{2,1,0:T(8,128)}, u32[]{:S(2)}) copy-start(f32[2,512,2048]{2,1,0:T(8,128)} %get-tuple-element.325) | copy-start | bytes 25165828 | tf_op jit(solution)/shard_map/while
  152.7 3.3 copy-start.1
  169.8 6.4 %copy-start.2 = (bf16[1,512,2,128]{3,2,1,0:T(2,128)(2,1)S(1)}, bf16[1,512,2,128]{3,2,1,0:T(2,128)(2,1)}, u32[]{:S(2)}) copy-start(bf16[1,512,2,128]{3,2,1,0:T(2,128)(2,1)} %get-tuple-element.327) | copy-start | bytes 786436 | tf_op jit(solution)/shard_map/while
  169.8 6.4 %copy-start.8 = (bf16[2048,128]{1,0:T(8,128)(2,1)S(1)}, bf16[2048,128]{1,0:T(8,128)(2,1)}, u32[]{:S(2)}) copy-start(bf16[2048,128]{1,0:T(8,128)(2,1)} %get-tuple-element.366) | copy-start | bytes 1572868 | tf_op jit(solution)/shard_map/while
  169.8 6.4 %copy-start.15 = (f32[2,512,2048]{2,1,0:T(8,128)S(1)}, f32[2,512,2048]{2,1,0:T(8,128)}, u32[]{:S(2)}) copy-start(f32[2,512,2048]{2,1,0:T(8,128)} %get-tuple-element.325) | copy-start | bytes 25165828 | tf_op jit(solution)/shard_map/while
  177.7 3.3 copy-start.1
  194.9 6.4 %copy-start.2 = (bf16[1,512,2,128]{3,2,1,0:T(2,128)(2,1)S(1)}, bf16[1,512,2,128]{3,2,1,0:T(2,128)(2,1)}, u32[]{:S(2)}) copy-start(bf16[1,512,2,128]{3,2,1,0:T(2,128)(2,1)} %get-tuple-element.327) | copy-start | bytes 786436 | tf_op jit(solution)/shard_map/while
  194.9 6.4 %copy-start.8 = (bf16[2048,128]{1,0:T(8,128)(2,1)S(1)}, bf16[2048,128]{1,0:T(8,128)(2,1)}, u32[]{:S(2)}) copy-start(bf16[2048,128]{1,0:T(8,128)(2,1)} %get-tuple-element.366) | copy-start | bytes 1572868 | tf_op jit(solution)/shard_map/while
  194.9 6.4 %copy-start.15 = (f32[2,512,2048]{2,1,0:T(8,128)S(1)}, f32[2,512,2048]{2,1,0:T(8,128)}, u32[]{:S(2)}) copy-start(f32[2,512,2048]{2,1,0:T(8,128)} %get-tuple-element.325) | copy-start | bytes 25165828 | tf_op jit(solution)/shard_map/while
  202.8 3.3 copy-start.1
  208.0 11.2 %copy-start.12 = (s32[8,1]{0,1:T(1,128)S(1)}, s32[8,1]{0,1:T(1,128)}, u32[]{:S(2)}) copy-start(s32[8,1]{0,1:T(1,128)} %copy-done.11) | copy-start | bytes 100
  208.0 11.2 %copy-start.14 = (s32[1,8]{1,0:T(1,128)S(1)}, s32[1,8]{1,0:T(1,128)}, u32[]{:S(2)}) copy-start(s32[1,8]{1,0:T(1,128)} %param.19) | copy-start | bytes 100
  211.8 15.2 %all-to-all-start.7 = ((bf16[16,2,8192]{2,1,0:T(2,128)(2,1)}), bf16[16,2,8192]{2,1,0:T(2,128)(2,1)S(1)}, u32[]{:S(2)}, u32[]{:S(2)}) async-start(bf16[16,2,8192]{2,1,0:T(2,128)(2,1)} %reshape.230), calls=%async_computation.7 | async-start | bytes 1048576 | tf_op jit(solution)/shard_map/all_to_all | solution.py:110
  227.0 32.2 %all-to-all-start.6 = ((bf16[16,2,8192]{2,1,0:T(2,128)(2,1)}), bf16[16,2,8192]{2,1,0:T(2,128)(2,1)}, u32[]{:S(2)}, u32[]{:S(2)}) async-start(bf16[16,2,8192]{2,1,0:T(2,128)(2,1)} %reshape.228), calls=%async_computation.6 | async-start | bytes 1048576 | tf_op jit(solution)/shard_map/all_to_all | solution.py:109
  233.3 274.0 %all-reduce.3.cloned.1.call-start = ((), (), s32[]{:S(2)}) async-start(), calls=%async_computation.8 | async-start | bytes 5767168 | tf_op jit(solution)/shard_map/psum | solution.py:137
  234.3 3.4 copy-start.5
  259.2 19.6 %all-to-all-start.5 = ((bf16[16,2,16384]{2,1,0:T(2,128)(2,1)}), bf16[16,2,16384]{2,1,0:T(2,128)(2,1)}, u32[]{:S(2)}, u32[]{:S(2)}) async-start(bf16[16,2,16384]{2,1,0:T(2,128)(2,1)} %reshape.226), calls=%async_computation.5 | async-start | bytes 2097152 | tf_op jit(solution)/shard_map/all_to_all | solution.py:104
  507.3 3.3 copy-start.9
Sparse Core Ops, SparseCore 0:
  240.2 266.9 all-reduce.2
where the time goes:
time: 520 us; the launch traced here: 518 us
  waiting for transfers between devices  277 us (53%)
  matrix products  81.9 us (16%)
  local copies, waits for them, and re-layouts  67 us (13%)
  starting transfers between devices  51.3 us (10%)
  other arithmetic  26.1 us (5%)
  between operations  14.3 us (3%)
    psum x1, waiting for transfers between devices, per_device(): lax.psum((down_portion, up_portion), ('grp', 'seq'))  220 us
    sub x4, matrix products, block_step(): weights = jnp.exp(masked - top)  29.4 us
    unnamed x41, local copies, waits for them, and re-layouts  26.3 us
    dot_general x4, matrix products, block_step(): jnp.einsum('hqk,qhd->kd', prob.astype(jnp.bfloat16), u_block, preferred_e...  25.1 us
    all_to_all x1, waiting for transfers between devices, per_device(): lax.all_to_all(u_slots, 'seq', split_axis=1, concat_axis=0, tiled=True)  12.6 us
    all_to_all x1, waiting for transfers between devices, per_device(): lax.all_to_all(q_slots, 'seq', split_axis=1, concat_axis=0, tiled=True)  12.1 us
    reshape x1, other arithmetic, per_device(): dquery = dquery.reshape(span, 1, per_tenant_slot * HEAD_SIZE)  11.6 us
    dynamic_slice x12, local copies, waits for them, and re-layouts, per_device(): lax.scan(block_step, (empty, empty), block_items)  11.1 us
  transfers between devices with their start and end apart: 9, of which 7 were waited for; matrix products, arithmetic and copies ran while one was open for 12% of the time, Pallas kernels for 0%

commit v1 on v0

v1 whole, which is shorter than its diff:
```python
import functools
import math

import jax
import jax.numpy as jnp
from jax import lax
from jax.experimental import pallas as pl
from jax.experimental.pallas import tpu as pltpu
from jax.sharding import PartitionSpec as P

HEAD_SIZE = 128
ADAPTER_RANK = 16
TENANTS = 8
DOCS = 8
SLOTS = 16
TOK = 128
BACK = 8
CHUNKS = BACK + 1
PAIRS = 16
SCALE = HEAD_SIZE**-0.5
LOG2E_SCALE = SCALE * math.log2(math.e)
NEG = -1e30
F32 = jnp.float32
BF16 = jnp.bfloat16
VMEM_LIMIT = 40 * 1024 * 1024

adapter_scale = 2.0


def dot_nt(a, b):
    return lax.dot_general(a, b, (((1,), (1,)), ((), ())), preferred_element_type=F32)


def dot(a, b):
    return jnp.dot(a, b, preferred_element_type=F32)


def doc_rows(len_ref, ten_ref, pos):
    begin = jnp.int32(0)
    start = jnp.zeros_like(pos)
    tenant = jnp.zeros_like(pos)
    for d in range(DOCS):
        inside = pos >= begin
        start = jnp.where(inside, begin, start)
        tenant = jnp.where(inside, ten_ref[0, d], tenant)
        begin = begin + len_ref[0, d]
    return start, tenant


def chunk_positions(chunk):
    return chunk * TOK + lax.broadcasted_iota(jnp.int32, (1, TOK), 1)


def fold(full, tenant):
    out = jnp.zeros((ADAPTER_RANK, TOK), F32)
    for t in range(TENANTS):
        out = out + jnp.where(tenant == t, full[t * ADAPTER_RANK : (t + 1) * ADAPTER_RANK], 0.0)
    return out


def expand(rows, tenant):
    return jnp.concatenate([jnp.where(tenant == t, rows, 0.0) for t in range(TENANTS)], axis=0)


def fill_bias(len_ref, ten_ref, me, bias):
    query = chunk_positions(me)
    start, _ = doc_rows(len_ref, ten_ref, query)
    for c in range(CHUNKS):
        key = (me - c) * TOK + lax.broadcasted_iota(jnp.int32, (TOK, TOK), 0)
        bias[c] = jnp.where((key >= start) & (key <= query), 0.0, NEG)


def pair_rows(ref, p):
    at = pl.multiple_of(p * 256, 256)
    return jnp.concatenate([ref[:, pl.ds(at, 128)], ref[:, pl.ds(at + 128, 128)]], axis=0)


def prep_kernel(len_ref, ten_ref, x_ref, d_ref, u_ref, o_ref, low_ref, delta_ref):
    me = lax.axis_index("seq")
    low = dot(x_ref[...], d_ref[...])
    _, tenant = doc_rows(len_ref, ten_ref, chunk_positions(me))
    low_ref[...] = fold(low.T, tenant).astype(BF16)
    for h in range(2 * PAIRS):
        lanes = slice(h * 128, (h + 1) * 128)
        product = u_ref[:, lanes].astype(F32) * o_ref[:, lanes].astype(F32)
        row = jnp.sum(product.T, axis=0, keepdims=True)
        delta_ref[h // 2 : h // 2 + 1, (h % 2) * 128 : (h % 2 + 1) * 128] = row


def values_kernel(len_ref, ten_ref, q_ref, u_ref, low_ref, up_ref, *refs):
    k_refs, refs = refs[:CHUNKS], refs[CHUNKS:]
    dv_refs, refs = refs[:CHUNKS], refs[CHUNKS:]
    slots_ref, upart_ref, m_ref, rl_ref, bias, weights, acc = refs
    me = lax.axis_index("seq")
    fill_bias(len_ref, ten_ref, me, bias)
    acc[...] = jnp.zeros_like(acc)

    def pair(p, carry):
        queries, upstream = pair_rows(q_ref, p), pair_rows(u_ref, p)
        lanes = pl.ds(pl.multiple_of((p // 4) * 128, 128), 128)
        top = jnp.full((8, 256), NEG, F32)
        for c in range(CHUNKS):
            s = dot_nt(k_refs[c][:, lanes], queries)
            b = bias[c]
            s = s + jnp.concatenate([b, b], axis=1)
            weights[c] = s
            top = jnp.maximum(top, jnp.max(s.reshape(16, 8, 256), axis=0))
        top = jnp.max(top, axis=0, keepdims=True)
        total = jnp.zeros((8, 256), F32)
        for c in range(CHUNKS):
            e = jnp.exp2((weights[c] - top) * LOG2E_SCALE)
            weights[c] = e
            total = total + jnp.sum(e.reshape(16, 8, 256), axis=0)
        inverse = 1.0 / jnp.sum(total, axis=0, keepdims=True)
        for c in range(CHUNKS):
            prob = (weights[c] * inverse).astype(BF16)
            acc[c, :, lanes] += dot(prob, upstream)
        m_ref[pl.ds(p, 1), :] = top
        rl_ref[pl.ds(p, 1), :] = inverse
        return carry

    lax.fori_loop(0, PAIRS, pair, 0)
    slots_ref[...] = jnp.zeros_like(slots_ref)
    upart = jnp.zeros(upart_ref.shape, F32)
    for c in range(CHUNKS):
        dv = acc[c].astype(BF16)
        dv_refs[c][...] = dv
        _, tenant = doc_rows(len_ref, ten_ref, chunk_positions(me - c))
        owner = lax.rem(me - c + SLOTS, SLOTS)
        back = dot_nt(up_ref[...], dv) * adapter_scale
        slots_ref[owner] = fold(back, tenant).astype(BF16)
        low = expand(low_ref[owner].astype(F32), tenant).astype(BF16)
        upart = upart + dot(low, dv)
    upart_ref[...] = upart * adapter_scale


def keys_kernel(len_ref, ten_ref, q_ref, u_ref, m_ref, rl_ref, delta_ref, *refs):
    k_refs, refs = refs[:CHUNKS], refs[CHUNKS:]
    v_refs, refs = refs[:CHUNKS], refs[CHUNKS:]
    dq_ref, refs = refs[0], refs[1:]
    dk_refs, refs = refs[:CHUNKS], refs[CHUNKS:]
    bias, dscores, key_t, acc = refs
    me = lax.axis_index("seq")
    fill_bias(len_ref, ten_ref, me, bias)
    acc[...] = jnp.zeros_like(acc)
    for kv in range(4):
        for c in range(CHUNKS):
            key_t[kv, :, c * 128 : (c + 1) * 128] = (
                k_refs[c][:, kv * 128 : (kv + 1) * 128].astype(F32).T.astype(BF16)
            )

    def pair(p, carry):
        queries, upstream = pair_rows(q_ref, p), pair_rows(u_ref, p)
        kv = p // 4
        lanes = pl.ds(pl.multiple_of(kv * 128, 128), 128)
        top = m_ref[pl.ds(p, 1), :]
        inverse = rl_ref[pl.ds(p, 1), :]
        delta = delta_ref[pl.ds(p, 1), :]
        for c in range(CHUNKS):
            b = bias[c]
            s = dot_nt(k_refs[c][:, lanes], queries) + jnp.concatenate([b, b], axis=1)
            prob = jnp.exp2((s - top) * LOG2E_SCALE) * inverse
            dprob = dot_nt(v_refs[c][:, lanes], upstream)
            dscore = (prob * (dprob - delta)).astype(BF16)
            dscores[c * 128 : (c + 1) * 128, :] = dscore
            acc[c, :, lanes] += dot(dscore, queries)
        dq = (dot(key_t[kv], dscores[...]) * SCALE).T.astype(BF16)
        at = pl.multiple_of(p * 256, 256)
        dq_ref[:, pl.ds(at, 128)] = dq[:128]
        dq_ref[:, pl.ds(at + 128, 128)] = dq[128:]
        return carry

    lax.fori_loop(0, PAIRS, pair, 0)
    for c in range(CHUNKS):
        dk_refs[c][...] = (acc[c] * SCALE).astype(BF16)


def maps_kernel(len_ref, ten_ref, x_ref, slots_ref, upart_ref, keep_ref, send_ref):
    me = lax.axis_index("seq")
    core = lax.rem(lax.axis_index("grp"), 2)
    _, tenant = doc_rows(len_ref, ten_ref, chunk_positions(me))
    rows = jnp.zeros((ADAPTER_RANK, TOK), F32)
    for j in range(SLOTS):
        rows = rows + slots_ref[j].astype(F32)
    back = expand(rows, tenant).astype(BF16)
    half = keep_ref.shape[1]
    width = x_ref.shape[1]

    def halves(first, second):
        first[...] = dot(back, x_ref[:, :half]).astype(BF16)
        second[:, : width - half] = dot(back, x_ref[:, half:]).astype(BF16)
        second[:, width - half :] = upart_ref[...].astype(BF16)

    pl.when(core == 0)(lambda: halves(keep_ref, send_ref))
    pl.when(core == 1)(lambda: halves(send_ref, keep_ref))


def final_kernel(mine_ref, other_ref, down_ref, up_ref):
    core = lax.rem(lax.axis_index("grp"), 2)
    half = mine_ref.shape[1]
    width = down_ref.shape[0]

    def write(first, second):
        for at in range(0, width, 128):
            ref, base = (first, at) if at < half else (second, at - half)
            down_ref[at : at + 128, :] = ref[:, base : base + 128].astype(F32).T
        up_ref[...] = second[:, width - half :].astype(F32)

    pl.when(core == 0)(lambda: write(mine_ref, other_ref))
    pl.when(core == 1)(lambda: write(other_ref, mine_ref))


def call(kernel, out_shape, n_in, scratch=()):
    smem = pl.BlockSpec(memory_space=pltpu.SMEM)
    vmem = pl.BlockSpec(memory_space=pltpu.VMEM)
    n_smem = 0 if kernel is final_kernel else 2
    return pl.pallas_call(
        kernel,
        out_shape=out_shape,
        in_specs=[smem] * n_smem + [vmem] * n_in,
        out_specs=jax.tree.map(lambda _: vmem, out_shape),
        scratch_shapes=list(scratch),
        compiler_params=pltpu.CompilerParams(vmem_limit_bytes=VMEM_LIMIT),
    )


def shape(dims, dtype):
    return jax.ShapeDtypeStruct(dims, dtype)


def shifted(array, by):
    return lax.ppermute(array, "seq", [(i, (i + by) % SLOTS) for i in range(SLOTS)])


def swap(array, distance):
    count = lax.axis_size("grp")
    return lax.ppermute(array, "grp", [(i, i ^ distance) for i in range(count)])


def spread(array):
    return lax.all_to_all(array, "seq", split_axis=0, concat_axis=0, tiled=True)


def after(array, *others):
    return lax.optimization_barrier((array,) + others)[0]


def per_device(
    inputs,
    queries,
    keys,
    values,
    outputs,
    upstream,
    lengths,
    tenants,
    adapter_down_maps,
    adapter_up_maps,
):
    x, q, k, v, o, u = (a[0] for a in (inputs, queries, keys, values, outputs, upstream))
    width, kv_width = x.shape[1], k.shape[1]
    half = (width + kv_width) // 2
    ranks = TENANTS * ADAPTER_RANK

    k_chunks = [k] + [shifted(k, s) for s in range(1, CHUNKS)]
    low, delta = call(
        prep_kernel,
        (shape((ADAPTER_RANK, TOK), BF16), shape((PAIRS, 256), F32)),
        4,
    )(lengths, tenants, x, adapter_down_maps, u, o)
    low_all = spread(jnp.broadcast_to(low[None], (SLOTS, ADAPTER_RANK, TOK)))

    part = shape((TOK, kv_width), BF16)
    bias = pltpu.VMEM((CHUNKS, TOK, TOK), F32)
    acc = pltpu.VMEM((CHUNKS, TOK, kv_width), F32)
    *dv_parts, slots, upart, top, inverse = call(
        values_kernel,
        (part,) * CHUNKS
        + (
            shape((SLOTS, ADAPTER_RANK, TOK), BF16),
            shape((ranks, kv_width), F32),
            shape((PAIRS, 256), F32),
            shape((PAIRS, 256), F32),
        ),
        4 + CHUNKS,
        (bias, pltpu.VMEM((CHUNKS, TOK, 256), F32), acc),
    )(lengths, tenants, q, u, low_all, adapter_up_maps, *k_chunks)

    v_late = after(v, *k_chunks)
    v_chunks = [v] + [shifted(v_late, s) for s in range(1, CHUNKS)]

    slots = spread(slots)
    keep, send = call(
        maps_kernel,
        (shape((ranks, half), BF16), shape((ranks, half), BF16)),
        3,
    )(lengths, tenants, x, slots, upart)
    got = swap(send, 1)
    mixed = (keep.astype(F32) + got.astype(F32)).astype(BF16)
    mixed = spread(mixed.reshape(SLOTS, ranks // SLOTS, half))

    dq, *dk_parts = call(
        keys_kernel,
        (shape(q.shape, BF16),) + (part,) * CHUNKS,
        5 + 2 * CHUNKS,
        (
            bias,
            pltpu.VMEM((CHUNKS * TOK, 256), BF16),
            pltpu.VMEM((kv_width // 128, 128, CHUNKS * TOK), BF16),
            acc,
        ),
    )(lengths, tenants, q, u, top, inverse, delta, *k_chunks, *v_chunks)

    dv_home = [dv_parts[0]] + [shifted(dv_parts[s], -s) for s in range(1, CHUNKS)]
    dk_home = [dk_parts[0]] + [shifted(dk_parts[s], -s) for s in range(1, CHUNKS)]
    values_gradient = functools.reduce(jnp.add, [a.astype(F32) for a in dv_home]).astype(BF16)
    keys_gradient = functools.reduce(jnp.add, [a.astype(F32) for a in dk_home]).astype(BF16)

    total = jnp.sum(mixed.astype(F32), axis=0)
    distance = 2
    while distance < lax.axis_size("grp"):
        short = lax.optimization_barrier(total.astype(BF16))
        total = short.astype(F32) + swap(short, distance).astype(F32)
        distance *= 2
    total = lax.optimization_barrier(total.astype(BF16))
    mine = spread(jnp.broadcast_to(total[None], (SLOTS, ranks // SLOTS, half)))
    mine = mine.reshape(ranks, half)
    other = swap(mine, 1)
    down, up = call(
        final_kernel,
        (shape((width, ranks), F32), shape((ranks, kv_width), F32)),
        2,
    )(mine, other)
    return dq[None], keys_gradient[None], values_gradient[None], down, up


def solution(mesh):
    in_specs = (
        P("grp", "seq", None),
        P("grp", "seq", None),
        P("grp", "seq", None),
        P("grp", "seq", None),
        P("grp", "seq", None),
        P("grp", "seq", None),
        P("grp", None),
        P("grp", None),
        P(),
        P(),
    )
    out_specs = (P("grp", "seq", None), P("grp", "seq", None), P("grp", "seq", None), P(), P())
    return jax.shard_map(
        per_device, mesh=mesh, in_specs=in_specs, out_specs=out_specs, check_vma=False
    )
```

time: 520 us -> 239 us (0.46)
  waiting for transfers between devices: 277 us -> 19 us
  matrix products: 81.9 us -> 0 us
  Pallas kernels: 0 us -> 50.3 us
  starting transfers between devices: 51.3 us -> 93.9 us
  blocking collectives: 0 us -> 41.7 us
  local copies, waits for them, and re-layouts: 67 us -> 28.2 us
  other arithmetic: 26.1 us -> 4.51 us
  between operations: 14.3 us -> 0.99 us
    psum x1 -> x0, waiting for transfers between devices: 220 us -> none  [per_device(): lax.psum((down_portion, up_portion), ('grp', 'seq'))]
    ppermute x0 -> x37, starting transfers between devices: none -> 88.4 us  [the longest x32 75.8 us: shifted(): lax.ppermute(array, 'seq', [(i, (i + by) % SLOTS) for i in range(SLOTS)])]
    all_to_all x8 -> x1, waiting for transfers between devices: 56.9 us -> 0.01 us  [spread(): return lax.all_to_all(array, 'seq', split_axis=0, concat_axis=0, tiled=True)]
    dot_general x18 -> x0, matrix products: 52.5 us -> none  [the longest x4 25.1 us: block_step(): jnp.einsum('hqk,qhd->kd', prob.astype(jnp.bfloat16), u_block, preferred_e...]
    pallas_call x0 -> x5, Pallas kernels: none -> 50.3 us  [the longest x1 30.8 us: per_device(): call(keys_kernel, (shape(q.shape, BF16),) + (part,) * CHUNKS, 5 + 2 * CHU...]
    all_to_all x8 -> x1, starting transfers between devices: 51.3 us -> 5.57 us  [spread(): return lax.all_to_all(array, 'seq', split_axis=0, concat_axis=0, tiled=True)]
    all_to_all x0 -> x3, blocking collectives: none -> 41.7 us  [spread(): return lax.all_to_all(array, 'seq', split_axis=0, concat_axis=0, tiled=True)]
    sub x4 -> x0, matrix products: 29.4 us -> none  [block_step(): weights = jnp.exp(masked - top)]
  transfers between devices with their start and end apart: 9 -> 38, of which waited for: 7 -> 8; matrix products, arithmetic and copies ran while one was open for 12% -> 1% of each run, Pallas kernels for 0% -> 13%
where the time goes in v1:
time: 239 us
  starting transfers between devices  93.9 us (39%)
  Pallas kernels  50.3 us (21%)
  blocking collectives  41.7 us (17%)
  local copies, waits for them, and re-layouts  28.2 us (12%)
  waiting for transfers between devices  19 us (8%)
  other arithmetic  4.51 us (2%)
    ppermute x32, starting transfers between devices, shifted(): lax.ppermute(array, 'seq', [(i, (i + by) % SLOTS) for i in range(SLOTS)])  75.8 us
    all_to_all x3, blocking collectives, spread(): return lax.all_to_all(array, 'seq', split_axis=0, concat_axis=0, tiled=True)  41.7 us
    pallas_call x1, Pallas kernels, per_device(): call(keys_kernel, (shape(q.shape, BF16),) + (part,) * CHUNKS, 5 + 2 * CHU...  30.8 us
    unnamed x108, local copies, waits for them, and re-layouts  27.2 us
    pallas_call x1, Pallas kernels, per_device(): call(values_kernel, (part,) * CHUNKS + (shape((SLOTS, ADAPTER_RANK, TOK),...  15.2 us
    ppermute x5, starting transfers between devices, swap(): return lax.ppermute(array, 'grp', [(i, i ^ distance) for i in range(count)])  12.6 us
    ppermute x32, waiting for transfers between devices, shifted(): lax.ppermute(array, 'seq', [(i, (i + by) % SLOTS) for i in range(SLOTS)])  10.3 us
    ppermute x5, waiting for transfers between devices, swap(): return lax.ppermute(array, 'grp', [(i, i ^ distance) for i in range(count)])  8.7 us
  transfers between devices with their start and end apart: 38, of which 8 were waited for; matrix products, arithmetic and copies ran while one was open for 1% of the time, Pallas kernels for 13%

profile of v1, /device:TPU:2, one launch (start us, length us, event | category | flops | bytes accessed | tf_op | source)
XLA Modules:
  0.0 238.6 jit_solution(2181587053998882650)
XLA Ops:
  0.6 2.2 collective-permute-start.7
  2.8 2.3 collective-permute-start.6
  5.2 3.1 %collective-permute-start.5 = (bf16[128,512]{1,0:T(8,128)(2,1)}, bf16[128,512]{1,0:T(8,128)(2,1)S(1)}, u32[]{:S(2)}, u32[]{:S(2)}) collective-permute-start(bf16[128,512]{1,0:T(8,128)(2,1)} %bitcast.26), channel_id=1, source_target_pairs={{0,6},{1,7},{2,8},{3,9},{4,10},{5,11},{6,12},{7,13},{8,14},{9,15},... | collective-permute-start | bytes 393224 | tf_op jit(solution)/shard_map/ppermute | solution.py:232
  8.3 1.6 collective-permute-start.4
  10.3 2.6 %collective-permute-start.2 = (bf16[128,512]{1,0:T(8,128)(2,1)}, bf16[128,512]{1,0:T(8,128)(2,1)S(1)}, u32[]{:S(2)}, u32[]{:S(2)}) collective-permute-start(bf16[128,512]{1,0:T(8,128)(2,1)} %bitcast.29), channel_id=1, source_target_pairs={{0,3},{1,4},{2,5},{3,6},{4,7},{5,8},{6,9},{7,10},{8,11},{9,12},{10... | collective-permute-start | bytes 393224 | tf_op jit(solution)/shard_map/ppermute | solution.py:232
  12.9 2.9 %collective-permute-start.1 = (bf16[128,512]{1,0:T(8,128)(2,1)}, bf16[128,512]{1,0:T(8,128)(2,1)S(1)}, u32[]{:S(2)}, u32[]{:S(2)}) collective-permute-start(bf16[128,512]{1,0:T(8,128)(2,1)} %bitcast.30), channel_id=1, source_target_pairs={{0,2},{1,3},{2,4},{3,5},{4,6},{5,7},{6,8},{7,9},{8,10},{9,11},{10,... | collective-permute-start | bytes 393224 | tf_op jit(solution)/shard_map/ppermute | solution.py:232
  17.4 1.2 copy-done
  18.6 1.3 copy-done.2
  19.9 1.3 copy-done.5
  21.3 1.2 copy-done.6
  23.8 1.2 shard_map.137
  25.1 14.1 %all_to_all.20.low_ref = bf16[16,16,128]{2,1,0:T(8,128)(2,1)S(1)} all-to-all(bf16[16,16,128]{2,1,0:T(8,128)(2,1)S(1)} %broadcast_in_dim.10), channel_id=1, replica_groups=mesh['grp'=16,'seq'=16] {'seq'}, dimensions={0} | all-to-all | bytes 131072 | tf_op jit(solution)/shard_map/all_to_all | solution.py:241
  39.3 15.2 %shard_map.138 = (bf16[128,512]{1,0:T(8,128)(2,1)S(1)}, bf16[128,512]{1,0:T(8,128)(2,1)S(1)}, bf16[128,512]{1,0:T(8,128)(2,1)S(1)}, bf16[128,512]{1,0:T(8,128)(2...) custom-call(s32[1,8]{1,0:T(1,128)S(1)} %copy-done.37, ...), custom_call_target="tpu_custom_call" | custom-call | tf_op jit(solution)/shard_map/pallas_call | solution.py:276
  58.5 10.9 %all_to_all.21.slots_ref = bf16[16,16,128]{2,1,0:T(8,128)(2,1)S(1)} all-to-all(bf16[16,16,128]{2,1,0:T(8,128)(2,1)S(1)} %get-tuple-element.59), channel_id=1, replica_groups=mesh['grp'=16,'seq'=16] {'seq'}, dimensions={0} | all-to-all | bytes 131072 | tf_op jit(solution)/shard_map/all_to_all | solution.py:241
  70.5 2.2 collective-permute-done.32
  72.9 16.8 %all_to_all.22 = bf16[16,8,2816]{2,1,0:T(8,128)(2,1)S(1)} all-to-all(bf16[16,8,2816]{2,1,0:T(8,128)(2,1)S(1)} %fusion), channel_id=1, replica_groups=mesh['grp'=16,'seq'=16] {'seq'}, dimensions={0} | all-to-all | bytes 1441792 | tf_op jit(solution)/shard_map/all_to_all | solution.py:241
  90.4 1.9 collective-permute-start.33
  92.3 2.3 collective-permute-done.33
  95.5 3.6 %collective-permute-start.34 = (bf16[8,2816]{1,0:T(8,128)(2,1)S(1)}, bf16[8,2816]{1,0:T(8,128)(2,1)S(1)}, u32[]{:S(2)}, u32[]{:S(2)}) collective-permute-start(bf16[8,2816]{1,0:T(8,128)(2,1)S(1)} %add_convert_fusion.5), channel_id=1, source_target_pairs={{0,64},{16,80},{32,96},{48,112},{64,0},{80,16},{96,32},{112,48},{1... | collective-permute-start | bytes 135176 | tf_op jit(solution)/shard_map/ppermute | solution.py:237
  99.0 2.0 collective-permute-done.34
  101.1 6.9 %collective-permute-start.35 = (bf16[8,2816]{1,0:T(8,128)(2,1)S(1)}, bf16[8,2816]{1,0:T(8,128)(2,1)S(1)}, u32[]{:S(2)}, u32[]{:S(2)}) collective-permute-start(bf16[8,2816]{1,0:T(8,128)(2,1)S(1)} %add_convert_fusion.4), channel_id=1, source_target_pairs={{0,128},{16,144},{32,160},{48,176},{64,192},{80,208},{96,224},{112... | collective-permute-start | bytes 135176 | tf_op jit(solution)/shard_map/ppermute | solution.py:237
  108.0 2.2 collective-permute-done.35
  111.1 5.6 %all-to-all-start.3 = ((bf16[16,8,2816]{2,1,0:T(8,128)(2,1)}), bf16[16,8,2816]{2,1,0:T(8,128)(2,1)S(1)}, u32[]{:S(2)}, u32[]{:S(2)}) async-start(bf16[16,8,2816]{2,1,0:T(8,128)(2,1)} %broadcast_in_dim.25), calls=%async_computation.3 | async-start | bytes 1441792 | tf_op jit(solution)/shard_map/all_to_all | solution.py:241
  116.6 2.1 collective-permute-start.15
  118.7 2.1 collective-permute-start.14
  120.8 3.3 %collective-permute-start.13 = (bf16[128,512]{1,0:T(8,128)(2,1)}, bf16[128,512]{1,0:T(8,128)(2,1)S(1)}, u32[]{:S(2)}, u32[]{:S(2)}) collective-permute-start(bf16[128,512]{1,0:T(8,128)(2,1)} %bitcast.36), channel_id=1, source_target_pairs={{0,6},{1,7},{2,8},{3,9},{4,10},{5,11},{6,12},{7,13},{8,14},{9,15},... | collective-permute-start | bytes 393224 | tf_op jit(solution)/shard_map/ppermute | solution.py:232
  124.0 1.5 collective-permute-start.12
  126.7 6.2 %collective-permute-start.10 = (bf16[128,512]{1,0:T(8,128)(2,1)}, bf16[128,512]{1,0:T(8,128)(2,1)S(1)}, u32[]{:S(2)}, u32[]{:S(2)}) collective-permute-start(bf16[128,512]{1,0:T(8,128)(2,1)} %bitcast.39), channel_id=1, source_target_pairs={{0,3},{1,4},{2,5},{3,6},{4,7},{5,8},{6,9},{7,10},{8,11},{9,12},{10... | collective-permute-start | bytes 393224 | tf_op jit(solution)/shard_map/ppermute | solution.py:232
  133.5 2.7 %collective-permute-start.9 = (bf16[128,512]{1,0:T(8,128)(2,1)}, bf16[128,512]{1,0:T(8,128)(2,1)S(1)}, u32[]{:S(2)}, u32[]{:S(2)}) collective-permute-start(bf16[128,512]{1,0:T(8,128)(2,1)} %bitcast.40), channel_id=1, source_target_pairs={{0,2},{1,3},{2,4},{3,5},{4,6},{5,7},{6,8},{7,9},{8,10},{9,11},{10,... | collective-permute-start | bytes 393224 | tf_op jit(solution)/shard_map/ppermute | solution.py:232
  138.5 3.1 %collective-permute-start.24 = (bf16[128,512]{1,0:T(8,128)(2,1)}, bf16[128,512]{1,0:T(8,128)(2,1)S(1)}, u32[]{:S(2)}, u32[]{:S(2)}) collective-permute-start(bf16[128,512]{1,0:T(8,128)(2,1)} %copy-done.47), channel_id=1, source_target_pairs={{0,15},{1,0},{2,1},{3,2},{4,3},{5,4},{6,5},{7,6},{8,7},{9,8},{10,9... | collective-permute-start | bytes 393224 | tf_op jit(solution)/shard_map/ppermute | solution.py:232
  142.3 2.6 %collective-permute-start.25 = (bf16[128,512]{1,0:T(8,128)(2,1)}, bf16[128,512]{1,0:T(8,128)(2,1)S(1)}, u32[]{:S(2)}, u32[]{:S(2)}) collective-permute-start(bf16[128,512]{1,0:T(8,128)(2,1)} %copy-done.46), channel_id=1, source_target_pairs={{0,14},{1,15},{2,0},{3,1},{4,2},{5,3},{6,4},{7,5},{8,6},{9,7},{10,... | collective-permute-start | bytes 393224 | tf_op jit(solution)/shard_map/ppermute | solution.py:232
  145.6 3.1 %collective-permute-start.26 = (bf16[128,512]{1,0:T(8,128)(2,1)}, bf16[128,512]{1,0:T(8,128)(2,1)S(1)}, u32[]{:S(2)}, u32[]{:S(2)}) collective-permute-start(bf16[128,512]{1,0:T(8,128)(2,1)} %copy-done.45), channel_id=1, source_target_pairs={{0,13},{1,14},{2,15},{3,0},{4,1},{5,2},{6,3},{7,4},{8,5},{9,6},{10... | collective-permute-start | bytes 393224 | tf_op jit(solution)/shard_map/ppermute | solution.py:232
  150.0 1.3 collective-permute-start.28
  151.3 5.8 %collective-permute-start.29 = (bf16[128,512]{1,0:T(8,128)(2,1)}, bf16[128,512]{1,0:T(8,128)(2,1)}, u32[]{:S(2)}, u32[]{:S(2)}) collective-permute-start(bf16[128,512]{1,0:T(8,128)(2,1)} %copy-done.42), channel_id=1, source_target_pairs={{0,10},{1,11},{2,12},{3,13},{4,14},{5,15},{6,0},{7,1},{8,2},{9,3},... | collective-permute-start | bytes 393224 | tf_op jit(solution)/shard_map/ppermute | solution.py:232
  157.1 2.9 %collective-permute-start.31 = (bf16[128,512]{1,0:T(8,128)(2,1)}, bf16[128,512]{1,0:T(8,128)(2,1)}, u32[]{:S(2)}, u32[]{:S(2)}) collective-permute-start(bf16[128,512]{1,0:T(8,128)(2,1)} %copy-done.40), channel_id=1, source_target_pairs={{0,8},{1,9},{2,10},{3,11},{4,12},{5,13},{6,14},{7,15},{8,0},{9,1},... | collective-permute-start | bytes 393224 | tf_op jit(solution)/shard_map/ppermute | solution.py:232
  171.9 30.8 %shard_map.139 = (bf16[128,4096]{1,0:T(8,128)(2,1)}, bf16[128,512]{1,0:T(8,128)(2,1)S(1)}, bf16[128,512]{1,0:T(8,128)(2,1)S(1)}, bf16[128,512]{1,0:T(8,128)(2,1)...) custom-call(s32[1,8]{1,0:T(1,128)S(1)} %copy-done.37, ...), custom_call_target="tpu_custom_call" | custom-call | tf_op jit(solution)/shard_map/pallas_call | solution.py:302
  202.7 3.3 %collective-permute-start.16 = (bf16[128,512]{1,0:T(8,128)(2,1)S(1)}, bf16[128,512]{1,0:T(8,128)(2,1)S(1)}, u32[]{:S(2)}, u32[]{:S(2)}) collective-permute-start(bf16[128,512]{1,0:T(8,128)(2,1)S(1)} %get-tuple-element.42), channel_id=1, source_target_pairs={{0,15},{1,0},{2,1},{3,2},{4,3},{5,4},{6,5},{7,6},{8,7},{9,8},{10,9... | collective-permute-start | bytes 393224 | tf_op jit(solution)/shard_map/ppermute | solution.py:232
  205.9 1.2 collective-permute-start.17
  207.2 2.4 %collective-permute-start.18 = (bf16[128,512]{1,0:T(8,128)(2,1)S(1)}, bf16[128,512]{1,0:T(8,128)(2,1)S(1)}, u32[]{:S(2)}, u32[]{:S(2)}) collective-permute-start(bf16[128,512]{1,0:T(8,128)(2,1)S(1)} %get-tuple-element.44), channel_id=1, source_target_pairs={{0,13},{1,14},{2,15},{3,0},{4,1},{5,2},{6,3},{7,4},{8,5},{9,6},{10... | collective-permute-start | bytes 393224 | tf_op jit(solution)/shard_map/ppermute | solution.py:232
  209.5 3.7 %collective-permute-start.19 = (bf16[128,512]{1,0:T(8,128)(2,1)S(1)}, bf16[128,512]{1,0:T(8,128)(2,1)S(1)}, u32[]{:S(2)}, u32[]{:S(2)}) collective-permute-start(bf16[128,512]{1,0:T(8,128)(2,1)S(1)} %get-tuple-element.45), channel_id=1, source_target_pairs={{0,12},{1,13},{2,14},{3,15},{4,0},{5,1},{6,2},{7,3},{8,4},{9,5},{1... | collective-permute-start | bytes 393224 | tf_op jit(solution)/shard_map/ppermute | solution.py:232
  213.2 4.7 %collective-permute-start.20 = (bf16[128,512]{1,0:T(8,128)(2,1)S(1)}, bf16[128,512]{1,0:T(8,128)(2,1)S(1)}, u32[]{:S(2)}, u32[]{:S(2)}) collective-permute-start(bf16[128,512]{1,0:T(8,128)(2,1)S(1)} %get-tuple-element.46), channel_id=1, source_target_pairs={{0,11},{1,12},{2,13},{3,14},{4,15},{5,0},{6,1},{7,2},{8,3},{9,4},{... | collective-permute-start | bytes 393224 | tf_op jit(solution)/shard_map/ppermute | solution.py:232
  217.9 2.7 %collective-permute-start.21 = (bf16[128,512]{1,0:T(8,128)(2,1)S(1)}, bf16[128,512]{1,0:T(8,128)(2,1)S(1)}, u32[]{:S(2)}, u32[]{:S(2)}) collective-permute-start(bf16[128,512]{1,0:T(8,128)(2,1)S(1)} %get-tuple-element.47), channel_id=1, source_target_pairs={{0,10},{1,11},{2,12},{3,13},{4,14},{5,15},{6,0},{7,1},{8,2},{9,3},... | collective-permute-start | bytes 393224 | tf_op jit(solution)/shard_map/ppermute | solution.py:232
  221.0 3.3 %collective-permute-start.23 = (bf16[128,512]{1,0:T(8,128)(2,1)S(1)}, bf16[128,512]{1,0:T(8,128)(2,1)S(1)}, u32[]{:S(2)}, u32[]{:S(2)}) collective-permute-start(bf16[128,512]{1,0:T(8,128)(2,1)S(1)} %get-tuple-element.49), channel_id=1, source_target_pairs={{0,8},{1,9},{2,10},{3,11},{4,12},{5,13},{6,14},{7,15},{8,0},{9,1},... | collective-permute-start | bytes 393224 | tf_op jit(solution)/shard_map/ppermute | solution.py:232
  224.3 2.0 fusion.2
  226.3 1.1 collective-permute-done.21
  227.4 2.4 collective-permute-done.22
  229.8 6.0 %collective-permute-done.23 = bf16[128,512]{1,0:T(8,128)(2,1)S(1)} collective-permute-done((bf16[128,512]{1,0:T(8,128)(2,1)S(1)}, bf16[128,512]{1,0:T(8,128)(2,1)S(1)}, u32[]{:S(2)}, u32[]{:S(2)}) %collective-permute-start.23) | collective-permute-done | bytes 131104 | tf_op jit(solution)/shard_map/ppermute | solution.py:232
  236.6 2.0 shard_map.141
  (153 shorter events, 30.9 us)
Async XLA Ops:
  0.6 9.7 %collective-permute-start.7 = (bf16[128,512]{1,0:T(8,128)(2,1)}, bf16[128,512]{1,0:T(8,128)(2,1)S(1)}, u32[]{:S(2)}, u32[]{:S(2)}) collective-permute-start(bf16[128,512]{1,0:T(8,128)(2,1)} %bitcast.24), channel_id=1, source_target_pairs={{0,8},{1,9},{2,10},{3,11},{4,12},{5,13},{6,14},{7,15},{8,0},{9,1},... | collective-permute-start | bytes 393224 | tf_op jit(solution)/shard_map/ppermute | solution.py:232
  2.8 10.1 %collective-permute-start.6 = (bf16[128,512]{1,0:T(8,128)(2,1)}, bf16[128,512]{1,0:T(8,128)(2,1)S(1)}, u32[]{:S(2)}, u32[]{:S(2)}) collective-permute-start(bf16[128,512]{1,0:T(8,128)(2,1)} %bitcast.25), channel_id=1, source_target_pairs={{0,7},{1,8},{2,9},{3,10},{4,11},{5,12},{6,13},{7,14},{8,15},{9,0},... | collective-permute-start | bytes 393224 | tf_op jit(solution)/shard_map/ppermute | solution.py:232
  5.2 11.4 %collective-permute-start.5 = (bf16[128,512]{1,0:T(8,128)(2,1)}, bf16[128,512]{1,0:T(8,128)(2,1)S(1)}, u32[]{:S(2)}, u32[]{:S(2)}) collective-permute-start(bf16[128,512]{1,0:T(8,128)(2,1)} %bitcast.26), channel_id=1, source_target_pairs={{0,6},{1,7},{2,8},{3,9},{4,10},{5,11},{6,12},{7,13},{8,14},{9,15},... | collective-permute-start | bytes 393224 | tf_op jit(solution)/shard_map/ppermute | solution.py:232
  8.3 30.9 %collective-permute-start.4 = (bf16[128,512]{1,0:T(8,128)(2,1)}, bf16[128,512]{1,0:T(8,128)(2,1)S(1)}, u32[]{:S(2)}, u32[]{:S(2)}) collective-permute-start(bf16[128,512]{1,0:T(8,128)(2,1)} %bitcast.27), channel_id=1, source_target_pairs={{0,5},{1,6},{2,7},{3,8},{4,9},{5,10},{6,11},{7,12},{8,13},{9,14},{... | collective-permute-start | bytes 393224 | tf_op jit(solution)/shard_map/ppermute | solution.py:232
  9.9 29.3 %collective-permute-start.3 = (bf16[128,512]{1,0:T(8,128)(2,1)}, bf16[128,512]{1,0:T(8,128)(2,1)S(1)}, u32[]{:S(2)}, u32[]{:S(2)}) collective-permute-start(bf16[128,512]{1,0:T(8,128)(2,1)} %bitcast.28), channel_id=1, source_target_pairs={{0,4},{1,5},{2,6},{3,7},{4,8},{5,9},{6,10},{7,11},{8,12},{9,13},{1... | collective-permute-start | bytes 393224 | tf_op jit(solution)/shard_map/ppermute | solution.py:232
  10.3 28.8 %collective-permute-start.2 = (bf16[128,512]{1,0:T(8,128)(2,1)}, bf16[128,512]{1,0:T(8,128)(2,1)S(1)}, u32[]{:S(2)}, u32[]{:S(2)}) collective-permute-start(bf16[128,512]{1,0:T(8,128)(2,1)} %bitcast.29), channel_id=1, source_target_pairs={{0,3},{1,4},{2,5},{3,6},{4,7},{5,8},{6,9},{7,10},{8,11},{9,12},{10... | collective-permute-start | bytes 393224 | tf_op jit(solution)/shard_map/ppermute | solution.py:232
  12.9 26.3 %collective-permute-start.1 = (bf16[128,512]{1,0:T(8,128)(2,1)}, bf16[128,512]{1,0:T(8,128)(2,1)S(1)}, u32[]{:S(2)}, u32[]{:S(2)}) collective-permute-start(bf16[128,512]{1,0:T(8,128)(2,1)} %bitcast.30), channel_id=1, source_target_pairs={{0,2},{1,3},{2,4},{3,5},{4,6},{5,7},{6,8},{7,9},{8,10},{9,11},{10,... | collective-permute-start | bytes 393224 | tf_op jit(solution)/shard_map/ppermute | solution.py:232
  16.6 22.7 %collective-permute-start = (bf16[128,512]{1,0:T(8,128)(2,1)}, bf16[128,512]{1,0:T(8,128)(2,1)S(1)}, u32[]{:S(2)}, u32[]{:S(2)}) collective-permute-start(bf16[128,512]{1,0:T(8,128)(2,1)} %bitcast.31), channel_id=1, source_target_pairs={{0,1},{1,2},{2,3},{3,4},{4,5},{5,6},{6,7},{7,8},{8,9},{9,10},{10,1... | collective-permute-start | bytes 393224 | tf_op jit(solution)/shard_map/ppermute | solution.py:232
  23.8 15.5 %copy-start.4 = (bf16[1,128,4096]{2,1,0:T(8,128)(2,1)S(1)}, bf16[1,128,4096]{2,1,0:T(8,128)(2,1)}, u32[]{:S(2)}) copy-start(bf16[1,128,4096]{2,1,0:T(8,128)(2,1)} %param.11) | copy-start | bytes 3145732
  23.8 15.5 %copy-start.7 = (bf16[1,128,512]{2,1,0:T(8,128)(2,1)S(1)}, bf16[1,128,512]{2,1,0:T(8,128)(2,1)}, u32[]{:S(2)}) copy-start(bf16[1,128,512]{2,1,0:T(8,128)(2,1)} %param.12) | copy-start | bytes 393220
  23.8 15.5 %copy-start.16 = (bf16[128,512]{1,0:T(8,128)(2,1)S(1)}, bf16[128,512]{1,0:T(8,128)(2,1)}, u32[]{:S(2)}) copy-start(bf16[128,512]{1,0:T(8,128)(2,1)} %up_ref.1) | copy-start | bytes 393220
  23.8 15.5 %copy-start.37 = (s32[1,8]{1,0:T(1,128)S(1)}, s32[1,8]{1,0:T(1,128)}, u32[]{:S(2)}) copy-start(s32[1,8]{1,0:T(1,128)} %len_ref.7) | copy-start | bytes 100
  23.8 15.5 %copy-start.39 = (s32[1,8]{1,0:T(1,128)S(1)}, s32[1,8]{1,0:T(1,128)}, u32[]{:S(2)}) copy-start(s32[1,8]{1,0:T(1,128)} %ten_ref.7) | copy-start | bytes 100
  39.3 30.1 %copy-start.3 = (bf16[1,128,5120]{2,1,0:T(8,128)(2,1)S(1)}, bf16[1,128,5120]{2,1,0:T(8,128)(2,1)}, u32[]{:S(2)}) copy-start(bf16[1,128,5120]{2,1,0:T(8,128)(2,1)} %param.10) | copy-start | bytes 3932164
  70.4 2.3 collective-permute-start.32
  90.4 4.3 %collective-permute-start.33 = (bf16[8,2816]{1,0:T(8,128)(2,1)}, bf16[8,2816]{1,0:T(8,128)(2,1)S(1)}, u32[]{:S(2)}, u32[]{:S(2)}) collective-permute-start(bf16[8,2816]{1,0:T(8,128)(2,1)} %reduce_sum.12), channel_id=1, source_target_pairs={{0,32},{16,48},{32,0},{48,16},{64,96},{80,112},{96,64},{112,80},{1... | collective-permute-start | bytes 135176 | tf_op jit(solution)/shard_map/ppermute | solution.py:237
  95.5 5.6 %collective-permute-start.34 = (bf16[8,2816]{1,0:T(8,128)(2,1)S(1)}, bf16[8,2816]{1,0:T(8,128)(2,1)S(1)}, u32[]{:S(2)}, u32[]{:S(2)}) collective-permute-start(bf16[8,2816]{1,0:T(8,128)(2,1)S(1)} %add_convert_fusion.5), channel_id=1, source_target_pairs={{0,64},{16,80},{32,96},{48,112},{64,0},{80,16},{96,32},{112,48},{1... | collective-permute-start | bytes 135176 | tf_op jit(solution)/shard_map/ppermute | solution.py:237
  101.1 9.1 %collective-permute-start.35 = (bf16[8,2816]{1,0:T(8,128)(2,1)S(1)}, bf16[8,2816]{1,0:T(8,128)(2,1)S(1)}, u32[]{:S(2)}, u32[]{:S(2)}) collective-permute-start(bf16[8,2816]{1,0:T(8,128)(2,1)S(1)} %add_convert_fusion.4), channel_id=1, source_target_pairs={{0,128},{16,144},{32,160},{48,176},{64,192},{80,208},{96,224},{112... | collective-permute-start | bytes 135176 | tf_op jit(solution)/shard_map/ppermute | solution.py:237
  111.1 49.0 %all-to-all-start.3 = ((bf16[16,8,2816]{2,1,0:T(8,128)(2,1)}), bf16[16,8,2816]{2,1,0:T(8,128)(2,1)S(1)}, u32[]{:S(2)}, u32[]{:S(2)}) async-start(bf16[16,8,2816]{2,1,0:T(8,128)(2,1)} %broadcast_in_dim.25), calls=%async_computation.3 | async-start | bytes 1441792 | tf_op jit(solution)/shard_map/all_to_all | solution.py:241
  116.6 9.4 %collective-permute-start.15 = (bf16[128,512]{1,0:T(8,128)(2,1)}, bf16[128,512]{1,0:T(8,128)(2,1)S(1)}, u32[]{:S(2)}, u32[]{:S(2)}) collective-permute-start(bf16[128,512]{1,0:T(8,128)(2,1)} %bitcast.34), channel_id=1, source_target_pairs={{0,8},{1,9},{2,10},{3,11},{4,12},{5,13},{6,14},{7,15},{8,0},{9,1},... | collective-permute-start | bytes 393224 | tf_op jit(solution)/shard_map/ppermute | solution.py:232
  118.7 14.2 %collective-permute-start.14 = (bf16[128,512]{1,0:T(8,128)(2,1)}, bf16[128,512]{1,0:T(8,128)(2,1)S(1)}, u32[]{:S(2)}, u32[]{:S(2)}) collective-permute-start(bf16[128,512]{1,0:T(8,128)(2,1)} %bitcast.35), channel_id=1, source_target_pairs={{0,7},{1,8},{2,9},{3,10},{4,11},{5,12},{6,13},{7,14},{8,15},{9,0},... | collective-permute-start | bytes 393224 | tf_op jit(solution)/shard_map/ppermute | solution.py:232
  120.8 15.4 %collective-permute-start.13 = (bf16[128,512]{1,0:T(8,128)(2,1)}, bf16[128,512]{1,0:T(8,128)(2,1)S(1)}, u32[]{:S(2)}, u32[]{:S(2)}) collective-permute-start(bf16[128,512]{1,0:T(8,128)(2,1)} %bitcast.36), channel_id=1, source_target_pairs={{0,6},{1,7},{2,8},{3,9},{4,10},{5,11},{6,12},{7,13},{8,14},{9,15},... | collective-permute-start | bytes 393224 | tf_op jit(solution)/shard_map/ppermute | solution.py:232
  124.0 13.8 %collective-permute-start.12 = (bf16[128,512]{1,0:T(8,128)(2,1)}, bf16[128,512]{1,0:T(8,128)(2,1)S(1)}, u32[]{:S(2)}, u32[]{:S(2)}) collective-permute-start(bf16[128,512]{1,0:T(8,128)(2,1)} %bitcast.37), channel_id=1, source_target_pairs={{0,5},{1,6},{2,7},{3,8},{4,9},{5,10},{6,11},{7,12},{8,13},{9,14},{... | collective-permute-start | bytes 393224 | tf_op jit(solution)/shard_map/ppermute | solution.py:232
  125.5 16.1 %collective-permute-start.11 = (bf16[128,512]{1,0:T(8,128)(2,1)}, bf16[128,512]{1,0:T(8,128)(2,1)S(1)}, u32[]{:S(2)}, u32[]{:S(2)}) collective-permute-start(bf16[128,512]{1,0:T(8,128)(2,1)} %bitcast.38), channel_id=1, source_target_pairs={{0,4},{1,5},{2,6},{3,7},{4,8},{5,9},{6,10},{7,11},{8,12},{9,13},{1... | collective-permute-start | bytes 393224 | tf_op jit(solution)/shard_map/ppermute | solution.py:232
  126.7 18.2 %collective-permute-start.10 = (bf16[128,512]{1,0:T(8,128)(2,1)}, bf16[128,512]{1,0:T(8,128)(2,1)S(1)}, u32[]{:S(2)}, u32[]{:S(2)}) collective-permute-start(bf16[128,512]{1,0:T(8,128)(2,1)} %bitcast.39), channel_id=1, source_target_pairs={{0,3},{1,4},{2,5},{3,6},{4,7},{5,8},{6,9},{7,10},{8,11},{9,12},{10... | collective-permute-start | bytes 393224 | tf_op jit(solution)/shard_map/ppermute | solution.py:232
  133.5 15.2 %collective-permute-start.9 = (bf16[128,512]{1,0:T(8,128)(2,1)}, bf16[128,512]{1,0:T(8,128)(2,1)S(1)}, u32[]{:S(2)}, u32[]{:S(2)}) collective-permute-start(bf16[128,512]{1,0:T(8,128)(2,1)} %bitcast.40), channel_id=1, source_target_pairs={{0,2},{1,3},{2,4},{3,5},{4,6},{5,7},{6,8},{7,9},{8,10},{9,11},{10,... | collective-permute-start | bytes 393224 | tf_op jit(solution)/shard_map/ppermute | solution.py:232
  136.8 12.5 %collective-permute-start.8 = (bf16[128,512]{1,0:T(8,128)(2,1)}, bf16[128,512]{1,0:T(8,128)(2,1)S(1)}, u32[]{:S(2)}, u32[]{:S(2)}) collective-permute-start(bf16[128,512]{1,0:T(8,128)(2,1)} %bitcast.41), channel_id=1, source_target_pairs={{0,1},{1,2},{2,3},{3,4},{4,5},{5,6},{6,7},{7,8},{8,9},{9,10},{10,1... | collective-permute-start | bytes 393224 | tf_op jit(solution)/shard_map/ppermute | solution.py:232
  138.5 12.8 %collective-permute-start.24 = (bf16[128,512]{1,0:T(8,128)(2,1)}, bf16[128,512]{1,0:T(8,128)(2,1)S(1)}, u32[]{:S(2)}, u32[]{:S(2)}) collective-permute-start(bf16[128,512]{1,0:T(8,128)(2,1)} %copy-done.47), channel_id=1, source_target_pairs={{0,15},{1,0},{2,1},{3,2},{4,3},{5,4},{6,5},{7,6},{8,7},{9,8},{10,9... | collective-permute-start | bytes 393224 | tf_op jit(solution)/shard_map/ppermute | solution.py:232
  142.3 14.8 %collective-permute-start.25 = (bf16[128,512]{1,0:T(8,128)(2,1)}, bf16[128,512]{1,0:T(8,128)(2,1)S(1)}, u32[]{:S(2)}, u32[]{:S(2)}) collective-permute-start(bf16[128,512]{1,0:T(8,128)(2,1)} %copy-done.46), channel_id=1, source_target_pairs={{0,14},{1,15},{2,0},{3,1},{4,2},{5,3},{6,4},{7,5},{8,6},{9,7},{10,... | collective-permute-start | bytes 393224 | tf_op jit(solution)/shard_map/ppermute | solution.py:232
  145.6 11.5 %collective-permute-start.26 = (bf16[128,512]{1,0:T(8,128)(2,1)}, bf16[128,512]{1,0:T(8,128)(2,1)S(1)}, u32[]{:S(2)}, u32[]{:S(2)}) collective-permute-start(bf16[128,512]{1,0:T(8,128)(2,1)} %copy-done.45), channel_id=1, source_target_pairs={{0,13},{1,14},{2,15},{3,0},{4,1},{5,2},{6,3},{7,4},{8,5},{9,6},{10... | collective-permute-start | bytes 393224 | tf_op jit(solution)/shard_map/ppermute | solution.py:232
  149.3 10.7 %collective-permute-start.27 = (bf16[128,512]{1,0:T(8,128)(2,1)}, bf16[128,512]{1,0:T(8,128)(2,1)}, u32[]{:S(2)}, u32[]{:S(2)}) collective-permute-start(bf16[128,512]{1,0:T(8,128)(2,1)} %copy-done.44), channel_id=1, source_target_pairs={{0,12},{1,13},{2,14},{3,15},{4,0},{5,1},{6,2},{7,3},{8,4},{9,5},{1... | collective-permute-start | bytes 393224 | tf_op jit(solution)/shard_map/ppermute | solution.py:232
  150.0 52.7 %collective-permute-start.28 = (bf16[128,512]{1,0:T(8,128)(2,1)}, bf16[128,512]{1,0:T(8,128)(2,1)}, u32[]{:S(2)}, u32[]{:S(2)}) collective-permute-start(bf16[128,512]{1,0:T(8,128)(2,1)} %copy-done.43), channel_id=1, source_target_pairs={{0,11},{1,12},{2,13},{3,14},{4,15},{5,0},{6,1},{7,2},{8,3},{9,4},{... | collective-permute-start | bytes 393224 | tf_op jit(solution)/shard_map/ppermute | solution.py:232
  151.3 54.6 %collective-permute-start.29 = (bf16[128,512]{1,0:T(8,128)(2,1)}, bf16[128,512]{1,0:T(8,128)(2,1)}, u32[]{:S(2)}, u32[]{:S(2)}) collective-permute-start(bf16[128,512]{1,0:T(8,128)(2,1)} %copy-done.42), channel_id=1, source_target_pairs={{0,10},{1,11},{2,12},{3,13},{4,14},{5,15},{6,0},{7,1},{8,2},{9,3},... | collective-permute-start | bytes 393224 | tf_op jit(solution)/shard_map/ppermute | solution.py:232
  157.1 50.1 %collective-permute-start.30 = (bf16[128,512]{1,0:T(8,128)(2,1)}, bf16[128,512]{1,0:T(8,128)(2,1)}, u32[]{:S(2)}, u32[]{:S(2)}) collective-permute-start(bf16[128,512]{1,0:T(8,128)(2,1)} %copy-done.41), channel_id=1, source_target_pairs={{0,9},{1,10},{2,11},{3,12},{4,13},{5,14},{6,15},{7,0},{8,1},{9,2},... | collective-permute-start | bytes 393224 | tf_op jit(solution)/shard_map/ppermute | solution.py:232
  157.1 52.4 %collective-permute-start.31 = (bf16[128,512]{1,0:T(8,128)(2,1)}, bf16[128,512]{1,0:T(8,128)(2,1)}, u32[]{:S(2)}, u32[]{:S(2)}) collective-permute-start(bf16[128,512]{1,0:T(8,128)(2,1)} %copy-done.40), channel_id=1, source_target_pairs={{0,8},{1,9},{2,10},{3,11},{4,12},{5,13},{6,14},{7,15},{8,0},{9,1},... | collective-permute-start | bytes 393224 | tf_op jit(solution)/shard_map/ppermute | solution.py:232
  160.0 76.6 %collective-permute-start.36 = (bf16[128,2816]{1,0:T(8,128)(2,1)S(1)}, bf16[128,2816]{1,0:T(8,128)(2,1)S(1)}, u32[]{:S(2)}, u32[]{:S(2)}) collective-permute-start(bf16[128,2816]{1,0:T(8,128)(2,1)S(1)} %bitcast.21), channel_id=1, source_target_pairs={{0,16},{16,0},{32,48},{48,32},{64,80},{80,64},{96,112},{112,96},{1... | collective-permute-start | bytes 2162696 | tf_op jit(solution)/shard_map/ppermute | solution.py:237
  171.9 52.4 %copy-start.19 = (bf16[128,512]{1,0:T(8,128)(2,1)S(1)}, bf16[128,512]{1,0:T(8,128)(2,1)}, u32[]{:S(2)}) copy-start(bf16[128,512]{1,0:T(8,128)(2,1)} %copy-done.18) | copy-start | bytes 393220
  171.9 52.4 %copy-start.49 = (bf16[128,512]{1,0:T(8,128)(2,1)S(1)}, bf16[128,512]{1,0:T(8,128)(2,1)}, u32[]{:S(2)}) copy-start(bf16[128,512]{1,0:T(8,128)(2,1)} %copy-done.48) | copy-start | bytes 393220
  171.9 52.4 %copy-start.51 = (bf16[128,512]{1,0:T(8,128)(2,1)S(1)}, bf16[128,512]{1,0:T(8,128)(2,1)}, u32[]{:S(2)}) copy-start(bf16[128,512]{1,0:T(8,128)(2,1)} %copy-done.50) | copy-start | bytes 393220
  171.9 52.4 %copy-start.53 = (bf16[128,512]{1,0:T(8,128)(2,1)S(1)}, bf16[128,512]{1,0:T(8,128)(2,1)}, u32[]{:S(2)}) copy-start(bf16[128,512]{1,0:T(8,128)(2,1)} %copy-done.52) | copy-start | bytes 393220
  202.7 10.5 %collective-permute-start.16 = (bf16[128,512]{1,0:T(8,128)(2,1)S(1)}, bf16[128,512]{1,0:T(8,128)(2,1)S(1)}, u32[]{:S(2)}, u32[]{:S(2)}) collective-permute-start(bf16[128,512]{1,0:T(8,128)(2,1)S(1)} %get-tuple-element.42), channel_id=1, source_target_pairs={{0,15},{1,0},{2,1},{3,2},{4,3},{5,4},{6,5},{7,6},{8,7},{9,8},{10,9... | collective-permute-start | bytes 393224 | tf_op jit(solution)/shard_map/ppermute | solution.py:232
  205.9 12.0 %collective-permute-start.17 = (bf16[128,512]{1,0:T(8,128)(2,1)S(1)}, bf16[128,512]{1,0:T(8,128)(2,1)S(1)}, u32[]{:S(2)}, u32[]{:S(2)}) collective-permute-start(bf16[128,512]{1,0:T(8,128)(2,1)S(1)} %get-tuple-element.43), channel_id=1, source_target_pairs={{0,14},{1,15},{2,0},{3,1},{4,2},{5,3},{6,4},{7,5},{8,6},{9,7},{10,... | collective-permute-start | bytes 393224 | tf_op jit(solution)/shard_map/ppermute | solution.py:232
  207.2 13.5 %collective-permute-start.18 = (bf16[128,512]{1,0:T(8,128)(2,1)S(1)}, bf16[128,512]{1,0:T(8,128)(2,1)S(1)}, u32[]{:S(2)}, u32[]{:S(2)}) collective-permute-start(bf16[128,512]{1,0:T(8,128)(2,1)S(1)} %get-tuple-element.44), channel_id=1, source_target_pairs={{0,13},{1,14},{2,15},{3,0},{4,1},{5,2},{6,3},{7,4},{8,5},{9,6},{10... | collective-permute-start | bytes 393224 | tf_op jit(solution)/shard_map/ppermute | solution.py:232
  209.5 11.4 %collective-permute-start.19 = (bf16[128,512]{1,0:T(8,128)(2,1)S(1)}, bf16[128,512]{1,0:T(8,128)(2,1)S(1)}, u32[]{:S(2)}, u32[]{:S(2)}) collective-permute-start(bf16[128,512]{1,0:T(8,128)(2,1)S(1)} %get-tuple-element.45), channel_id=1, source_target_pairs={{0,12},{1,13},{2,14},{3,15},{4,0},{5,1},{6,2},{7,3},{8,4},{9,5},{1... | collective-permute-start | bytes 393224 | tf_op jit(solution)/shard_map/ppermute | solution.py:232
  213.2 13.1 %collective-permute-start.20 = (bf16[128,512]{1,0:T(8,128)(2,1)S(1)}, bf16[128,512]{1,0:T(8,128)(2,1)S(1)}, u32[]{:S(2)}, u32[]{:S(2)}) collective-permute-start(bf16[128,512]{1,0:T(8,128)(2,1)S(1)} %get-tuple-element.46), channel_id=1, source_target_pairs={{0,11},{1,12},{2,13},{3,14},{4,15},{5,0},{6,1},{7,2},{8,3},{9,4},{... | collective-permute-start | bytes 393224 | tf_op jit(solution)/shard_map/ppermute | solution.py:232
  217.9 9.5 %collective-permute-start.21 = (bf16[128,512]{1,0:T(8,128)(2,1)S(1)}, bf16[128,512]{1,0:T(8,128)(2,1)S(1)}, u32[]{:S(2)}, u32[]{:S(2)}) collective-permute-start(bf16[128,512]{1,0:T(8,128)(2,1)S(1)} %get-tuple-element.47), channel_id=1, source_target_pairs={{0,10},{1,11},{2,12},{3,13},{4,14},{5,15},{6,0},{7,1},{8,2},{9,3},... | collective-permute-start | bytes 393224 | tf_op jit(solution)/shard_map/ppermute | solution.py:232
  220.7 9.1 %collective-permute-start.22 = (bf16[128,512]{1,0:T(8,128)(2,1)S(1)}, bf16[128,512]{1,0:T(8,128)(2,1)S(1)}, u32[]{:S(2)}, u32[]{:S(2)}) collective-permute-start(bf16[128,512]{1,0:T(8,128)(2,1)S(1)} %get-tuple-element.48), channel_id=1, source_target_pairs={{0,9},{1,10},{2,11},{3,12},{4,13},{5,14},{6,15},{7,0},{8,1},{9,2},... | collective-permute-start | bytes 393224 | tf_op jit(solution)/shard_map/ppermute | solution.py:232
  221.0 14.8 %collective-permute-start.23 = (bf16[128,512]{1,0:T(8,128)(2,1)S(1)}, bf16[128,512]{1,0:T(8,128)(2,1)S(1)}, u32[]{:S(2)}, u32[]{:S(2)}) collective-permute-start(bf16[128,512]{1,0:T(8,128)(2,1)S(1)} %get-tuple-element.49), channel_id=1, source_target_pairs={{0,8},{1,9},{2,10},{3,11},{4,12},{5,13},{6,14},{7,15},{8,0},{9,1},... | collective-permute-start | bytes 393224 | tf_op jit(solution)/shard_map/ppermute | solution.py:232
  (44 other events, 161.9 us)
